TPU v7x, 512 devices: a whole 4x8x8 slice. The times are simulated.
512 devices in a mesh: tm: 64 (over x, z_hi, y), head: 8 (over z_lo, core).
Axes of the slice: x: 4, y: 8, z: 8 (z_hi: 2, z_lo: 4; z = z_hi * 4 + z_lo), core: 2. Of those that a mesh axis runs over, the one named last changes fastest.
Arguments:
- queries: bfloat16 [8192, 3072], P('tm', 'head'), may hold values from -22 to 22
- keys: bfloat16 [8192, 3072], P('tm', 'head'), may hold values from -4 to 4
- values: bfloat16 [8192, 3072], P('tm', 'head'), may hold values from -5 to 5
- latents: bfloat16 [8192, 64], P('tm'), may hold values from -3 to 3
- out_weight: bfloat16 [3072, 64], P('head'), may hold values from -0.21875 to 0.21875
- step_size: float32 [64], replicated, may hold values from 0.5 to 2
- conv_weight: bfloat16 [3, 64, 512], P(None, None, 'head'), may hold values from -0.4375 to 0.4375
- span_of_slot: int32 [64], replicated, may hold values from 0 to 63, each once
- valid_count: int32 [64], replicated, may hold values from 32 to 128, as said below
- decoder_order: int32 [128], replicated, may hold values from 0 to 127, each once
Outputs:
- denoised: bfloat16 [128, 64, 64], P('tm')
- features: bfloat16 [128, 64, 512], P('tm', None, 'head')
Inputs may be any that keep to these rules, and one draw needn't show every extreme that they name: `valid_count`: at least one span is full and one holds 32 live tokens.
All inputs are finite; a program needn't handle non-finite values.
Results may differ from a plain program's by a relative error of at most 0.017.
Values may be sent and summed in bfloat16 or wider, within the bound.
A program may use at most 64 MiB of HBM per device.

v0:
```python
import jax
import jax.numpy as jnp
from jax import lax
from jax.sharding import PartitionSpec as P

HD = 128
KT = 3


def lookup_int(lookup_table, positions):
    matches = positions[:, None] == jnp.arange(lookup_table.shape[0], dtype=jnp.int32)[None, :]
    return jnp.sum(jnp.where(matches, lookup_table[None, :], 0), axis=1)


def lookup_float(lookup_table, positions):
    matches = positions[:, None] == jnp.arange(lookup_table.shape[0], dtype=jnp.int32)[None, :]
    return jnp.sum(jnp.where(matches, lookup_table[None, :], 0.0), axis=1)


def local(
    queries,
    keys,
    values,
    latents,
    out_weight,
    step_size,
    conv_weight,
    span_of_slot,
    valid_count,
    decoder_order,
):
    tok_dev = keys.shape[0]
    slot_count = lax.axis_size("tm")
    tile_rows = tok_dev // slot_count
    heads_here = keys.shape[1] // HD
    position = lax.axis_index("tm")
    permute = (span_of_slot[None, :] == jnp.arange(slot_count, dtype=jnp.int32)[:, None]).astype(
        jnp.bfloat16
    )
    got_queries, got_latents = (queries, latents)
    row_slot = jnp.zeros((tok_dev,), jnp.int32) + position
    row_span = lookup_int(span_of_slot, row_slot)
    row_token = jnp.arange(tok_dev, dtype=jnp.int32)
    group_count = 1
    row_live = row_token < lookup_int(valid_count, row_span)
    query_heads = got_queries.reshape(tok_dev, heads_here, HD)
    group_rows = tok_dev // group_count
    query_groups = [query_heads]
    span_groups = [row_span]
    group_tops = [jnp.max(span_part) for span_part in span_groups]
    score_scale = 1.0 / HD**0.5
    initial = tuple(
        (
            (
                jnp.full((heads_here, group_rows), -1e30, jnp.float32),
                jnp.zeros((heads_here, group_rows), jnp.float32),
                jnp.zeros((heads_here, group_rows, HD), jnp.float32),
            )
            for group in range(group_count)
        )
    )
    key_piece = lax.all_gather(keys, "tm", axis=0, tiled=True)
    value_piece = lax.all_gather(values, "tm", axis=0, tiled=True)
    piece_rows = key_piece.shape[0]

    def one_block(block_index, state):
        offset = block_index * tok_dev
        key_block = lax.dynamic_slice_in_dim(key_piece, offset, tok_dev, 0).reshape(
            tok_dev, heads_here, HD
        )
        value_block = lax.dynamic_slice_in_dim(value_piece, offset, tok_dev, 0).reshape(
            tok_dev, heads_here, HD
        )
        key_rows = offset + jnp.arange(tok_dev, dtype=jnp.int32)
        key_span = lookup_int(span_of_slot, key_rows // tok_dev)
        key_live = key_rows % tok_dev < lookup_int(valid_count, key_span)
        lowest = jnp.min(key_span)

        def update(inner, query_part=query_groups[0], span_part=span_groups[0]):
            row_max, row_total, weighted = inner
            scores = (
                jnp.einsum(
                    "qhd,khd->hqk", query_part, key_block, preferred_element_type=jnp.float32
                )
                * score_scale
            )
            allowed = key_live[None, :] & (key_span[None, :] <= span_part[:, None])
            scores = jnp.where(allowed[None], scores, -1e30)
            new_max = jnp.maximum(row_max, jnp.max(scores, axis=-1))
            weights = jnp.where(allowed[None], jnp.exp(scores - new_max[..., None]), 0.0)
            shrink = jnp.exp(row_max - new_max)
            row_total = row_total * shrink + jnp.sum(weights, axis=-1)
            product = jnp.einsum(
                "hqk,khd->hqd",
                weights.astype(jnp.bfloat16),
                value_block,
                preferred_element_type=jnp.float32,
            )
            weighted = weighted * shrink[..., None] + product
            return (new_max, row_total, weighted)

        def unchanged(inner):
            return inner

        new_state = [lax.cond(lowest <= group_tops[0], update, unchanged, state[0])]
        return tuple(new_state)

    finals = lax.fori_loop(0, piece_rows // tok_dev, one_block, initial)
    row_total = jnp.concatenate([item[1] for item in finals], axis=1)
    weighted = jnp.concatenate([item[2] for item in finals], axis=1)
    attended = weighted / row_total[..., None]
    attended = (
        jnp.transpose(attended, (1, 0, 2)).reshape(tok_dev, heads_here * HD).astype(jnp.bfloat16)
    )
    partial_velocity = jnp.dot(attended, out_weight, preferred_element_type=jnp.float32)
    velocity = lax.psum(partial_velocity.astype(jnp.bfloat16), "head").astype(jnp.float32)
    velocity = jnp.where(row_live[:, None], velocity, 0.0)
    row_step = lookup_float(step_size, row_span)
    updated = (got_latents.astype(jnp.float32) + row_step[:, None] * velocity).astype(jnp.bfloat16)
    ordered_updated = jnp.take(updated, decoder_order, axis=0)
    tile_data = lax.all_to_all(ordered_updated, "tm", split_axis=0, concat_axis=0, tiled=True)
    frames = tile_data.reshape(slot_count, tile_rows, tile_data.shape[1])
    denoised = jnp.einsum(
        "ts,spf->ptf", permute, frames, preferred_element_type=jnp.float32
    ).astype(jnp.bfloat16)
    padded = jnp.pad(denoised, ((0, 0), (KT - 1, 0), (0, 0)))
    features = jnp.zeros((tile_rows, slot_count, conv_weight.shape[2]), jnp.float32)
    for shift_back in range(KT):
        window = padded[:, KT - 1 - shift_back : KT - 1 - shift_back + slot_count, :]
        features = features + jnp.einsum(
            "ptf,fo->pto", window, conv_weight[shift_back], preferred_element_type=jnp.float32
        )
    return (denoised, features.astype(jnp.bfloat16))


def solution(mesh):
    return jax.shard_map(
        local,
        mesh=mesh,
        in_specs=(
            P("tm", "head"),
            P("tm", "head"),
            P("tm", "head"),
            P("tm", None),
            P("head", None),
            P(),
            P(None, None, "head"),
            P(),
            P(),
            P(),
        ),
        out_specs=(P("tm", None, None), P("tm", None, "head")),
        check_vma=False,
    )
```

profile of v0, /device:TPU:1, one launch (start us, length us, event | category | flops | bytes accessed | tf_op | source)
XLA Modules:
  0.0 837.9 jit_solution(17934056792131065258)
XLA Ops:
  16.1 209.4 %all-gather.3.cloned.1.call-done = bf16[8192,384]{0,1:T(8,128)(2,1)} async-done(((bf16[128,384]{0,1:T(8,128)(2,1)}), bf16[8192,384]{0,1:T(8,128)(2,1)}) %all-gather.3.cloned.1.call-update) | async-done | bytes 6291472 | tf_op jit(solution)/shard_map/all_gather | solution.py:62
  225.5 207.5 %all-gather.5.cloned.1.call-done = bf16[8192,384]{0,1:T(8,128)(2,1)} async-done(((bf16[128,384]{0,1:T(8,128)(2,1)}), bf16[8192,384]{0,1:T(8,128)(2,1)}) %all-gather.5.cloned.1.call-update) | async-done | bytes 6291472 | tf_op jit(solution)/shard_map/all_gather | solution.py:63
  433.1 279.5 %while.19 = (s32[]{:T(128)}, f32[3,128]{1,0:T(4,128)S(1)}, f32[3,128]{1,0:T(4,128)S(1)}, f32[3,128,128]{2,1,0:T(8,128)S(1)}, s32[64]{0:T(128)}, /*index=5*/s32[]...) while((s32[]{:T(128)}, f32[3,128]{1,0:T(4,128)S(1)}, ...), condition=%wide.region_12.13_spmd, body=%wide.region_4.12_spmd.sunk | while | flops 25792648 | bytes 1900177 | solution.py:108
  436.1 2.6 conditional.2
  441.6 2.6 conditional.2
  447.1 2.6 conditional.2
  467.1 2.6 conditional.2
  472.6 2.6 conditional.2
  487.0 2.6 conditional.2
  501.0 2.6 conditional.2
  515.5 2.6 conditional.2
  526.5 2.6 conditional.2
  532.1 2.6 conditional.2
  540.6 2.6 conditional.2
  549.1 2.6 conditional.2
  560.1 2.6 conditional.2
  565.6 2.6 conditional.2
  574.1 2.6 conditional.2
  579.7 2.6 conditional.2
  594.1 2.6 conditional.2
  619.6 2.6 conditional.2
  634.0 2.6 conditional.2
  642.5 2.6 conditional.2
  648.0 2.6 conditional.2
  653.6 2.6 conditional.2
  662.1 2.6 conditional.2
  673.1 2.6 conditional.2
  678.6 2.6 conditional.2
  687.1 2.6 conditional.2
  701.2 2.6 conditional.2
  713.0 23.8 %psum.7 = bf16[128,64]{0,1:T(8,128)(2,1)S(1)} all-reduce(bf16[128,64]{0,1:T(8,128)(2,1)S(1)} %convolution_convert_fusion.1), channel_id=1, replica_groups=mesh['tm'=64,'head'=8] {'head'}, use_global_device_ids=true, to_apply=%region_13.14 | all-reduce | flops 8192 | bytes 32768 | tf_op jit(solution)/shard_map/psum | solution.py:116
  737.8 90.3 %all_to_all.6 = bf16[64,2,64]{2,1,0:T(2,128)(2,1)S(1)} all-to-all(bf16[64,2,64]{2,1,0:T(2,128)(2,1)S(1)} %broadcast_select_fusion), channel_id=1, replica_groups=mesh['tm'=64,'head'=8] {'tm'}, dimensions={0} | all-to-all | bytes 32768 | tf_op jit(solution)/shard_map/all_to_all | solution.py:121
  (810 shorter events, 221.9 us)
Async XLA Ops:
  7.2 705.7 %copy-start = (bf16[384,64]{0,1:T(8,128)(2,1)S(1)}, bf16[384,64]{0,1:T(8,128)(2,1)}, u32[]{:S(2)}) copy-start(bf16[384,64]{0,1:T(8,128)(2,1)} %param.18) | copy-start | bytes 147460
  7.2 218.4 %all-gather.3.cloned.1.call-start = ((), (), s32[]{:S(2)}) async-start(), calls=%async_computation.1 | async-start | bytes 6389760 | tf_op jit(solution)/shard_map/all_gather | solution.py:62
  8.9 424.2 %all-gather.5.cloned.1.call-start = ((), (), s32[]{:S(2)}) async-start(), calls=%async_computation.2 | async-start | bytes 6389760 | tf_op jit(solution)/shard_map/all_gather | solution.py:63
  10.6 726.3 %copy-start.2 = (bf16[128,64]{0,1:T(8,128)(2,1)S(1)}, bf16[128,64]{0,1:T(8,128)(2,1)}, u32[]{:S(2)}) copy-start(bf16[128,64]{0,1:T(8,128)(2,1)} %param.17) | copy-start | bytes 49156
  433.1 396.6 %copy-start.1 = (bf16[3,64,64]{2,1,0:T(8,128)(2,1)S(1)}, bf16[3,64,64]{2,1,0:T(8,128)(2,1)}, u32[]{:S(2)}) copy-start(bf16[3,64,64]{2,1,0:T(8,128)(2,1)} %param.20) | copy-start | bytes 73732
Sparse Core Ops, SparseCore 0:
  12.3 213.1 all-gather.2
  229.8 203.1 all-gather.4
where the time goes:
time: 847 us; the launch traced here: 838 us
  waiting for transfers between devices  417 us (49%)
  other arithmetic  139 us (16%)
  blocking collectives  114 us (13%)
  loops' own time  91.8 us (11%)
  local copies, waits for them, and re-layouts  41.1 us (5%)
  matrix products  20.4 us (2%)
  between operations  14.1 us (2%)
    all_gather x1, waiting for transfers between devices, local(): key_piece = lax.all_gather(keys, 'tm', axis=0, tiled=True)  209 us
    all_gather x1, waiting for transfers between devices, local(): value_piece = lax.all_gather(values, 'tm', axis=0, tiled=True)  208 us
    all_to_all x1, blocking collectives, local(): lax.all_to_all(ordered_updated, 'tm', split_axis=0, concat_axis=0, tiled=...  90.3 us
    another operation x1, loops' own time, local(): finals = lax.fori_loop(0, piece_rows // tok_dev, one_block, initial)  88.9 us
    reduce_sum x101, other arithmetic, lookup_int(): return jnp.sum(jnp.where(matches, lookup_table[None, :], 0), axis=1)  83.3 us
    reduce_min x64, other arithmetic, one_block(): lowest = jnp.min(key_span)  45.4 us
    dynamic_slice x35, local copies, waits for them, and re-layouts, one_block(): lax.dynamic_slice_in_dim(value_piece, offset, tok_dev, 0)  33.7 us
    psum x1, blocking collectives, local(): lax.psum(partial_velocity.astype(jnp.bfloat16), 'head').astype(jnp.float32)  23.8 us
  transfers between devices with their start and end apart: 2, of which 2 were waited for; matrix products, arithmetic and copies ran while one was open for 1% of the time, Pallas kernels for 0%

commit v1 on v0

v1 whole, which is shorter than its diff:
```python
import jax
import jax.numpy as jnp
from jax import lax
from jax.experimental import pallas as pl
from jax.experimental.pallas import tpu as pltpu
from jax.sharding import PartitionSpec as P

HD = 128
HPD = 3
TOK = 128
LAT = 64
KT = 3
NX, NZ, NY = 4, 2, 8
NB = NX * NZ
NG = 8
PAIRS = TOK // 2
NSLOT = NB * NY
EXCLUDED = -1e30
SCALE = 1.4426950408889634 / HD**0.5
MESH = pl.DeviceIdType.MESH
QROWS = 256


def mod(value, size):
    return lax.rem(value + 2 * size, size)


def remote(src, dst, send, recv, device):
    return pltpu.make_async_remote_copy(
        src_ref=src, dst_ref=dst, send_sem=send, recv_sem=recv, device_id=device, device_id_type=MESH
    )


def kernel(
    q_ref, k_ref, v_ref, lat_ref, wout_ref, conv_ref, span_row_ref, order_ref,
    span_ref, valid_ref, step_ref,
    denoised_ref, features_ref,
    qbuf, kvbuf, vwbuf, obuf, lsebuf, sendbuf, c1buf, dbuf, ubuf, bias,
    q_send, q_recv, z_send, z_recv, x_send, x_recv, s_send, s_recv, c_send, c_recv, d_send, d_recv,
):
    tm = lax.axis_index("tm")
    g = lax.axis_index("head")
    b, a = lax.div(tm, NY), lax.rem(tm, NY)
    x, zh = lax.div(b, NZ), lax.rem(b, NZ)
    core = lax.rem(g, 2)
    way = 1 - 2 * core

    def slot_of(bb, aa):
        return bb * NY + aa

    y_next, y_prev = mod(a + way, NY), mod(a - way, NY)
    x_next, x_prev = mod(x + way, NX), mod(x - way, NX)
    to_y = {1: (slot_of(b, y_next), g), -1: (slot_of(b, y_prev), g)}
    to_x = {1: (slot_of(x_next * NZ + zh, a), g), -1: (slot_of(x_prev * NZ + zh, a), g)}
    b_other = x * NZ + 1 - zh
    to_z = (slot_of(b_other, a), g)
    self_last = b == g

    barrier = pltpu.get_barrier_semaphore()

    def greet(device):
        pl.semaphore_signal(barrier, inc=1, device_id=device, device_id_type=MESH)

    for device in (to_y[1], to_y[-1], to_x[1], to_x[-1], to_z):
        greet(device)
    for rel in range(1, NY * NG):
        greet((slot_of(b, mod(a + rel // NG, NY)), mod(g + rel % NG, NG)))
    for bb in range(NB):
        @pl.when(jnp.logical_not(jnp.logical_and(bb == b, self_last)))
        def _():
            greet((slot_of(bb, a), b))

    lane = lax.broadcasted_iota(jnp.int32, (TOK, TOK), 1)
    row = lax.broadcasted_iota(jnp.int32, (TOK, TOK), 0)
    order = order_ref[...].astype(jnp.float32)
    order_col = jnp.transpose(jnp.broadcast_to(order, (TOK, TOK)))
    pick = (order_col == lane.astype(jnp.float32)).astype(jnp.bfloat16)
    halves = (lane == 2 * lax.rem(row, PAIRS) + lax.div(row, PAIRS)).astype(jnp.bfloat16)
    pick = jnp.dot(halves, pick, preferred_element_type=jnp.float32).astype(jnp.bfloat16)
    order_row = lax.dot_general(
        jnp.broadcast_to(order, (8, TOK)).astype(jnp.bfloat16), halves, (((1,), (1,)), ((), ())),
        preferred_element_type=jnp.float32,
    )
    q_own = jnp.dot(pick, q_ref[...], preferred_element_type=jnp.float32).astype(jnp.bfloat16)
    for h in range(HPD):
        cols = slice(h * HD, (h + 1) * HD)
        qbuf[h, a] = q_own[:, cols]
        kvbuf[h, b, :TOK] = k_ref[:, cols]
        vw = jnp.dot(v_ref[:, cols], wout_ref[cols, :], preferred_element_type=jnp.float32)
        kvbuf[h, b, TOK:] = jnp.concatenate([vw[:PAIRS], vw[PAIRS:]], axis=1).astype(jnp.bfloat16)
    lat = jnp.dot(pick, lat_ref[...], preferred_element_type=jnp.float32)
    lat = jnp.concatenate([lat[:PAIRS], lat[PAIRS:]], axis=1)
    lat = jnp.where(g == 0, lat, 0.0)

    key_row = lax.broadcasted_iota(jnp.int32, (1, TOK), 1)
    my_spans = [span_ref[slot_of(b, i)] for i in range(NY)]
    for j in range(NB):
        key_span = span_ref[slot_of(j, a)]
        key_live = key_row < valid_ref[key_span]
        for i in range(NY):
            kept = jnp.logical_and(key_live, key_span <= my_spans[i])
            bias[i : i + 1, j * TOK : (j + 1) * TOK] = jnp.where(kept, 0.0, EXCLUDED)
    step_rows = jnp.concatenate(
        [
            jnp.where(order_row[0:1] < valid_ref[my_spans[i]].astype(jnp.float32), step_ref[my_spans[i]], 0.0)
            for i in range(NY)
        ],
        axis=0,
    )
    vwbuf[:, LAT:TOK] = jnp.zeros((NB * TOK, LAT), jnp.bfloat16)
    vwbuf[:, TOK:] = jnp.ones((NB * TOK, TOK), jnp.bfloat16)

    pl.semaphore_wait(barrier, 5 + NY * NG - 1 + NG - self_last.astype(jnp.int32))

    def q_copy(h, side, t):
        block = qbuf.at[h, mod(a - side * way * (t - 1), NY)]
        n = (0 if side == 1 else 4) + t - 1
        return remote(block, block, q_send.at[h, n], q_recv.at[h, n], to_y[side])

    def z_copy(h):
        block = kvbuf.at[h, b]
        return remote(block, block, z_send.at[h], z_recv.at[h], to_z)

    def x_copy(h, other, side, t):
        zz = 1 - zh if other else zh
        block = kvbuf.at[h, mod(x - side * way * (t - 1), NX) * NZ + zz]
        n = other * 3 + (0 if side == 1 else 2) + t - 1
        return remote(block, block, x_send.at[h, n], x_recv.at[h, n], to_x[side])

    started = []

    def start(copy):
        copy.start()
        started.append(copy)

    for h in range(HPD):
        start(z_copy(h))
        start(q_copy(h, 1, 1))
        start(q_copy(h, -1, 1))
        start(x_copy(h, 0, 1, 1))
        start(x_copy(h, 0, -1, 1))
    for h in range(HPD):
        q_copy(h, 1, 1).wait_recv()
        start(q_copy(h, 1, 2))
        q_copy(h, -1, 1).wait_recv()
        start(q_copy(h, -1, 2))
        x_copy(h, 0, 1, 1).wait_recv()
        start(x_copy(h, 0, 1, 2))
    for h in range(HPD):
        z_copy(h).wait_recv()
        start(x_copy(h, 1, 1, 1))
        start(x_copy(h, 1, -1, 1))
        q_copy(h, 1, 2).wait_recv()
        start(q_copy(h, 1, 3))
        q_copy(h, -1, 2).wait_recv()
        start(q_copy(h, -1, 3))
    for h in range(HPD):
        q_copy(h, 1, 3).wait_recv()
        start(q_copy(h, 1, 4))
        x_copy(h, 1, 1, 1).wait_recv()
        start(x_copy(h, 1, 1, 2))

    def lse_copy(h, rel):
        block = lsebuf.at[h, a]
        return remote(
            block, block, s_send.at[h, rel - 1], s_recv.at[h, rel - 1], (slot_of(b, mod(a + rel, NY)), g)
        )

    stat_lane = lax.broadcasted_iota(jnp.int32, (TOK, TOK), 1)
    for h in range(HPD):
        q_copy(h, 1, 4).wait_recv()
        q_copy(h, -1, 3).wait_recv()
        x_copy(h, 0, -1, 1).wait_recv()
        x_copy(h, 0, 1, 2).wait_recv()
        x_copy(h, 1, -1, 1).wait_recv()
        x_copy(h, 1, 1, 2).wait_recv()
        keys = kvbuf[h, :, :TOK].reshape(NB * TOK, HD)
        for j in range(NB):
            packed = kvbuf[h, j, TOK:]
            vwbuf[j * TOK : j * TOK + PAIRS, :LAT] = packed[:, :LAT]
            vwbuf[j * TOK + PAIRS : (j + 1) * TOK, :LAT] = packed[:, LAT:]
        vw = vwbuf[...]
        stats = jnp.zeros((TOK, TOK), jnp.float32)
        per = QROWS // TOK
        for i in range(NY // per):
            queries = qbuf[h, i * per : (i + 1) * per].reshape(QROWS, HD)
            scores = lax.dot_general(
                queries, keys, (((1,), (1,)), ((), ())), preferred_element_type=jnp.float32
            )
            scores = scores.reshape(per, TOK, NB * TOK) + bias[i * per : (i + 1) * per][:, None, :]
            scores = scores.reshape(QROWS, NB * TOK)
            top = jnp.max(scores, axis=1, keepdims=True)
            probs = jnp.exp2((scores - top) * SCALE).astype(jnp.bfloat16)
            out = jnp.dot(probs, vw, preferred_element_type=jnp.float32)
            total = out[:, TOK:]
            obuf[h, i * QROWS : (i + 1) * QROWS] = out[:, :TOK] / total
            lse = top * SCALE + jnp.log2(total)
            for p in range(per):
                stats = jnp.where(stat_lane == i * per + p, lse[p * TOK : (p + 1) * TOK], stats)
        lsebuf[h, a] = jnp.transpose(stats)[:NY]
        for rel in range(1, NY):
            start(lse_copy(h, rel))

    shares = []
    for h in range(HPD):
        for rel in range(1, NY):
            lse_copy(h, rel).wait_recv()
        parts = lsebuf[h]
        top = jnp.max(parts, axis=0)
        total = jnp.sum(jnp.exp2(parts - top[None]), axis=0)
        shares.append(jnp.exp2(lsebuf[h, a] - top) / total * step_rows)
    shares.append(jnp.zeros((TOK - HPD * NY, TOK), jnp.float32))
    share_cols = jnp.transpose(jnp.concatenate(shares, axis=0))
    terms = []
    for i in range(NY):
        rows = slice(i * TOK, (i + 1) * TOK)
        term = sum(obuf[h, rows] * share_cols[:, h * NY + i : h * NY + i + 1] for h in range(HPD))
        term = term[:PAIRS] + pltpu.roll(term[PAIRS:], LAT, 1)
        terms.append(term + jnp.where(a == i, lat, 0.0))
    sendbuf[...] = jnp.swapaxes(jnp.stack(terms, axis=0), 0, 1)

    def c_copy(rel):
        aa, gg = mod(a + rel // NG, NY), mod(g + rel % NG, NG)
        return remote(
            sendbuf.at[gg * NY + aa], c1buf.at[rel - 1], c_send, c_recv, (slot_of(b, aa), gg)
        )

    for rel in range(1, NY * NG):
        c_copy(rel).start()
    everything = remote(sendbuf.at[: NY * NG - 1], c1buf, c_send, c_recv, to_z)
    everything.wait_recv()
    ubuf[...] = sendbuf[g * NY + a] + jnp.sum(c1buf[...], axis=0)

    def d_copy(gg):
        return remote(ubuf, dbuf.at[b], d_send.at[gg], d_recv.at[b], (slot_of(g, a), gg))

    def own_target(gg):
        return jnp.logical_and(self_last, gg == g)

    for gg in range(NG):
        @pl.when(jnp.logical_not(own_target(gg)))
        def _():
            d_copy(gg).start()

    @pl.when(self_last)
    def _():
        dbuf[b] = ubuf[...]

    zeros = jnp.zeros((LAT, LAT), jnp.bfloat16)
    taps = []
    for k in range(KT):
        tap = conv_ref[k]
        taps.append(jnp.concatenate([tap, zeros], axis=1))
        taps.append(jnp.concatenate([zeros, tap], axis=1))
    taps = jnp.concatenate(taps, axis=0)
    time = lax.broadcasted_iota(jnp.int32, (NSLOT, NSLOT), 0)
    spans = jnp.broadcast_to(span_row_ref[...], (NSLOT, NSLOT))
    orders = [(spans == time - k).astype(jnp.bfloat16) for k in range(KT)]

    for bb in range(NB):
        @pl.when(jnp.logical_not(jnp.logical_and(self_last, bb == b)))
        def _():
            remote(ubuf, dbuf.at[bb], d_send.at[0], d_recv.at[bb], to_z).wait_recv()
    updated = dbuf[...].reshape(NSLOT, 2 * LAT).astype(jnp.bfloat16)
    shifted = [
        jnp.dot(order, updated, preferred_element_type=jnp.float32).astype(jnp.bfloat16) for order in orders
    ]
    features = jnp.dot(
        jnp.concatenate(shifted, axis=1), taps, preferred_element_type=jnp.float32
    ).astype(jnp.bfloat16)
    for p in range(2):
        denoised_ref[p] = shifted[0][:, p * LAT : (p + 1) * LAT]
        features_ref[p] = features[:, p * LAT : (p + 1) * LAT]

    for copy in started:
        copy.wait_send()
    everything.wait_send()
    for gg in range(NG):
        @pl.when(jnp.logical_not(own_target(gg)))
        def _():
            d_copy(gg).wait_send()


def local(
    queries, keys, values, latents, out_weight, step_size, conv_weight, span_of_slot, valid_count, decoder_order
):
    vmem, smem = pl.BlockSpec(memory_space=pltpu.VMEM), pl.BlockSpec(memory_space=pltpu.SMEM)
    dma = pltpu.SemaphoreType.DMA
    out = jax.ShapeDtypeStruct((2, NSLOT, LAT), jnp.bfloat16)
    return pl.pallas_call(
        kernel,
        out_shape=(out, out),
        in_specs=[vmem] * 8 + [smem] * 3,
        out_specs=(vmem, vmem),
        scratch_shapes=[
            pltpu.VMEM((HPD, NY, TOK, HD), jnp.bfloat16),
            pltpu.VMEM((HPD, NB, TOK + PAIRS, HD), jnp.bfloat16),
            pltpu.VMEM((NB * TOK, 2 * TOK), jnp.bfloat16),
            pltpu.VMEM((HPD, NY * TOK, TOK), jnp.float32),
            pltpu.VMEM((HPD, NY, NY, TOK), jnp.float32),
            pltpu.VMEM((PAIRS, NY, TOK), jnp.float32),
            pltpu.VMEM((NY * NG - 1, NY, TOK), jnp.float32),
            pltpu.VMEM((NB, NY, TOK), jnp.float32),
            pltpu.VMEM((NY, TOK), jnp.float32),
            pltpu.VMEM((NY, NB * TOK), jnp.float32),
            dma((HPD, 7)), dma((HPD, 7)),
            dma((HPD,)), dma((HPD,)),
            dma((HPD, 6)), dma((HPD, 6)),
            dma((HPD, NY - 1)), dma((HPD, NY - 1)),
            dma, dma,
            dma((NG,)), dma((NB,)),
        ],
        compiler_params=pltpu.CompilerParams(
            collective_id=0, has_side_effects=True, vmem_limit_bytes=48 * 2**20
        ),
        name="span_attention",
    )(
        queries, keys, values, latents, out_weight, conv_weight,
        span_of_slot.reshape(1, NSLOT), decoder_order.reshape(1, TOK),
        span_of_slot, valid_count, step_size,
    )


def solution(mesh):
    return jax.shard_map(
        local,
        mesh=mesh,
        in_specs=(
            P("tm", "head"),
            P("tm", "head"),
            P("tm", "head"),
            P("tm", None),
            P("head", None),
            P(),
            P(None, None, "head"),
            P(),
            P(),
            P(),
        ),
        out_specs=(P("tm", None, None), P("tm", None, "head")),
        check_vma=False,
    )
```

time: 847 us -> 63.4 us (0.07); the launches traced: 838 us -> 63.1 us
  waiting for transfers between devices: 417 us -> 0 us
  other arithmetic: 139 us -> 0 us
  blocking collectives: 114 us -> 0 us
  loops' own time: 91.8 us -> 0 us
  Pallas kernels: 0 us -> 57.7 us
  local copies, waits for them, and re-layouts: 41.1 us -> 4.74 us
  matrix products: 20.4 us -> 0 us
  between operations: 14.1 us -> 0.75 us
    all_gather x2 -> x0, waiting for transfers between devices: 417 us -> none  [the longest x1 209 us: local(): key_piece = lax.all_gather(keys, 'tm', axis=0, tiled=True)]
    another operation x65 -> x0, loops' own time: 91.8 us -> none  [the longest x1 88.9 us: local(): finals = lax.fori_loop(0, piece_rows // tok_dev, one_block, initial)]
    all_to_all x1 -> x0, blocking collectives: 90.3 us -> none  [local(): lax.all_to_all(ordered_updated, 'tm', split_axis=0, concat_axis=0, tiled=...]
    reduce_sum x137 -> x0, other arithmetic: 86.1 us -> none  [the longest x101 83.3 us: lookup_int(): return jnp.sum(jnp.where(matches, lookup_table[None, :], 0), axis=1)]
    pallas_call x0 -> x1, Pallas kernels: none -> 57.7 us  [local(): pl.pallas_call(kernel, out_shape=(out, out), in_specs=[vmem] * 8 + [smem]...]
    reduce_min x64 -> x0, other arithmetic: 45.4 us -> none  [one_block(): lowest = jnp.min(key_span)]
    dynamic_slice x35 -> x0, local copies, waits for them, and re-layouts: 33.7 us -> none  [one_block(): lax.dynamic_slice_in_dim(value_piece, offset, tok_dev, 0)]
    psum x1 -> x0, blocking collectives: 23.8 us -> none  [local(): lax.psum(partial_velocity.astype(jnp.bfloat16), 'head').astype(jnp.float32)]
  transfers between devices with their start and end apart: 2 -> 0, of which waited for: 2 -> 0; matrix products, arithmetic and copies ran while one was open for 1% -> 0% of each run, Pallas kernels for 0% -> 0%
where the time goes in v1:
time: 63.4 us; the launch traced here: 63.1 us
  Pallas kernels  57.7 us (91%)
  local copies, waits for them, and re-layouts  4.74 us (7%)
  between operations  0.75 us (1%)
    pallas_call x1, Pallas kernels, local(): pl.pallas_call(kernel, out_shape=(out, out), in_specs=[vmem] * 8 + [smem]...  57.7 us
    unnamed x20, local copies, waits for them, and re-layouts  4.74 us

profile of v1, /device:TPU:1, one launch (start us, length us, event | category | flops | bytes accessed | tf_op | source)
XLA Modules:
  0.0 63.1 jit_solution(6894941337549681151)
XLA Ops:
  0.6 0.0 copy-start.4
  0.6 0.0 copy-start.5
  0.7 0.0 copy-start.6
  0.7 0.0 copy-start.7
  0.7 0.0 copy-start
  0.7 0.0 copy-start.1
  0.7 0.9 %copy.12.lat_ref = bf16[128,64]{1,0:T(8,128)(2,1)S(1)} copy(bf16[128,64]{0,1:T(8,128)(2,1)} %param.13) | data formatting | bytes 32768 | tf_op args[3]
  1.6 0.9 %copy.13.wout_ref = bf16[384,64]{1,0:T(8,128)(2,1)S(1)} copy(bf16[384,64]{0,1:T(8,128)(2,1)} %param.14) | data formatting | bytes 98304 | tf_op args[4]
  2.5 0.0 copy-done.4
  2.5 0.0 copy-done.5
  2.5 0.0 copy-done.6
  2.5 0.0 copy-done.7
  2.5 0.0 copy-done
  2.5 0.0 copy-done.1
  2.6 0.0 copy-start.2
  2.6 0.9 %copy-done.2 = bf16[128,384]{1,0:T(8,128)(2,1)S(1)} copy-done((bf16[128,384]{1,0:T(8,128)(2,1)S(1)}, bf16[128,384]{1,0:T(8,128)(2,1)}, u32[]{:S(2)}) %copy-start.2) | copy-done | bytes 98328
  3.5 0.0 copy-start.3
  3.5 0.8 %copy-done.3 = bf16[3,64,64]{2,1,0:T(8,128)(2,1)S(1)} copy-done((bf16[3,64,64]{2,1,0:T(8,128)(2,1)S(1)}, bf16[3,64,64]{2,1,0:T(8,128)(2,1)}, u32[]{:S(2)}) %copy-start.3) | copy-done | bytes 24600
  4.3 57.7 %span_attention.1 = (bf16[2,64,64]{2,1,0:T(8,128)(2,1)S(1)}, bf16[2,64,64]{2,1,0:T(8,128)(2,1)S(1)}) custom-call(bf16[128,384]{1,0:T(8,128)(2,1)S(1)} %copy-done, bf16[128,384]{1,0:T(8,128)(2,1)S(1)} %copy-done.1, bf16[128,384]{1,0:T(8,128)(2,1)S(1)} %copy-done.2, bf16[128,64]{1,0:T(8,128)(2,1)S(1)} %copy.12.lat_ref, bf16[384,64]{1,0:T(8,128)(2,1)S(1)} %copy.13.wout_ref, ...), custom_call_target="tpu_custom_call" | custom-call | tf_op jit(solution)/shard_map/span_attention/pallas_call | solution.py:290
  61.9 0.6 copy.16
  62.5 0.6 copy.17
Async XLA Ops:
  0.6 1.9 %copy-start.4 = (s32[64]{0:T(128)S(1)}, s32[64]{0:T(128)}, u32[]{:S(2)}) copy-start(s32[64]{0:T(128)} %span_ref.1) | copy-start | bytes 772
  0.6 1.9 %copy-start.5 = (s32[128]{0:T(128)S(1)}, s32[128]{0:T(128)}, u32[]{:S(2)}) copy-start(s32[128]{0:T(128)} %param.19) | copy-start | bytes 1540
  0.7 1.9 %copy-start.6 = (s32[64]{0:T(128)S(1)}, s32[64]{0:T(128)}, u32[]{:S(2)}) copy-start(s32[64]{0:T(128)} %valid_ref.1) | copy-start | bytes 772
  0.7 1.9 %copy-start.7 = (f32[64]{0:T(128)S(1)}, f32[64]{0:T(128)}, u32[]{:S(2)}) copy-start(f32[64]{0:T(128)} %step_ref.1) | copy-start | bytes 772
  0.7 1.9 %copy-start = (bf16[128,384]{1,0:T(8,128)(2,1)S(1)}, bf16[128,384]{1,0:T(8,128)(2,1)}, u32[]{:S(2)}) copy-start(bf16[128,384]{1,0:T(8,128)(2,1)} %q_ref.1) | copy-start | bytes 294916
  0.7 1.9 %copy-start.1 = (bf16[128,384]{1,0:T(8,128)(2,1)S(1)}, bf16[128,384]{1,0:T(8,128)(2,1)}, u32[]{:S(2)}) copy-start(bf16[128,384]{1,0:T(8,128)(2,1)} %k_ref.1) | copy-start | bytes 294916
  2.6 0.9 %copy-start.2 = (bf16[128,384]{1,0:T(8,128)(2,1)S(1)}, bf16[128,384]{1,0:T(8,128)(2,1)}, u32[]{:S(2)}) copy-start(bf16[128,384]{1,0:T(8,128)(2,1)} %v_ref.1) | copy-start | bytes 294916
  3.5 0.8 %copy-start.3 = (bf16[3,64,64]{2,1,0:T(8,128)(2,1)S(1)}, bf16[3,64,64]{2,1,0:T(8,128)(2,1)}, u32[]{:S(2)}) copy-start(bf16[3,64,64]{2,1,0:T(8,128)(2,1)} %conv_ref.1) | copy-start | bytes 73732

commit v2 on v1

v2 whole, which is shorter than its diff:
```python
import jax
import jax.numpy as jnp
from jax import lax
from jax.experimental import pallas as pl
from jax.experimental.pallas import tpu as pltpu
from jax.sharding import PartitionSpec as P

HD = 128
HPD = 3
TOK = 128
LAT = 64
KT = 3
NX, NZ, NY = 4, 2, 8
NB = NX * NZ
NG = 8
NL = NG // 2
PAIRS = TOK // 2
NSLOT = NB * NY
HALF = NX * TOK
EXCLUDED = -1e30
SCALE = 1.4426950408889634 / HD**0.5
MESH = pl.DeviceIdType.MESH
ROWS_BY_KEYS = (((1,), (1,)), ((), ()))


def mod(value, size):
    return lax.rem(value + 2 * size, size)


def remote(src, dst, send, recv, device):
    return pltpu.make_async_remote_copy(
        src_ref=src, dst_ref=dst, send_sem=send, recv_sem=recv, device_id=device, device_id_type=MESH
    )


def dot(left, right, dims=(((1,), (0,)), ((), ()))):
    return lax.dot_general(left, right, dims, preferred_element_type=jnp.float32)


def kernel(
    q_hbm, k_hbm, v_hbm, lat_hbm, wout_hbm, conv_hbm, span_row_hbm, order_hbm, span_hbm, valid_hbm, step_hbm,
    denoised_ref, features_ref,
    v_ref, lat_ref, wout_ref, conv_ref, span_row_ref, order_ref, span_ref, valid_ref, step_ref,
    qbuf, kvbuf, vwbuf, acc, tops, obuf, bias, lsebuf, sendbuf, pairbuf, c1buf, ubuf, dbuf,
    ready, load, q_send, q_recv, z_send, z_recv, x_send, x_recv, s_send, s_recv,
    p_send, p_recv, c_send, c_recv, d_send, d_recv,
):
    tm = lax.axis_index("tm")
    g = lax.axis_index("head")
    b, a = lax.div(tm, NY), lax.rem(tm, NY)
    x, zh = lax.div(b, NZ), lax.rem(b, NZ)
    zl, core = lax.div(g, 2), lax.rem(g, 2)
    way = 1 - 2 * core

    def slot_of(bb, aa):
        return bb * NY + aa

    to_y = {s: (slot_of(b, mod(a + s * way, NY)), g) for s in (1, -1)}
    to_x = {s: (slot_of(mod(x + s, NX) * NZ + zh, a), g) for s in (1, -1, 2)}
    to_z = (slot_of(x * NZ + 1 - zh, a), g)
    to_core = (tm, g + way)
    self_last = b == g

    barrier = pltpu.get_barrier_semaphore()
    head_peers = [(tm, mod(g + rel, NG)) for rel in range(1, NG)]
    greeted = [to_z, to_x[1], to_x[-1], to_x[2], to_y[1], to_y[-1], *head_peers]
    for device in greeted:
        pl.semaphore_signal(barrier, inc=1, device_id=device, device_id_type=MESH)

    def partner(rel):
        return mod(a + rel // NL, NY), mod(zl + rel % NL, NL) * 2 + core

    loads = []

    def fetch(src, dst):
        copy = pltpu.make_async_copy(src, dst, load.at[len(loads)])
        copy.start()
        loads.append(copy)

    def cols(h):
        return slice(h * HD, (h + 1) * HD)

    fetch(v_hbm, v_ref)
    fetch(wout_hbm, wout_ref)
    for h in range(HPD):
        fetch(k_hbm.at[:, cols(h)], kvbuf.at[h, zh, x, :TOK])
    for h in range(HPD):
        fetch(q_hbm.at[:, cols(h)], qbuf.at[h, a])
    early = len(loads)
    for src, dst in (
        (span_hbm, span_ref), (valid_hbm, valid_ref), (step_hbm, step_ref), (span_row_hbm, span_row_ref),
        (order_hbm, order_ref), (lat_hbm, lat_ref), (conv_hbm, conv_ref),
    ):
        fetch(src, dst)
    for copy in loads[:2]:
        copy.wait()
    for h in range(HPD):
        vw = dot(v_ref[:, cols(h)], wout_ref[:, cols(h)], ROWS_BY_KEYS)
        kvbuf[h, zh, x, TOK:] = jnp.concatenate([vw[:PAIRS], vw[PAIRS:]], axis=1).astype(jnp.bfloat16)
    for copy in loads[2:early]:
        copy.wait()

    pl.semaphore_wait(barrier, len(greeted))

    def q_copy(h, side, t):
        block = qbuf.at[h, mod(a - side * way * (t - 1), NY)]
        n = (0 if side == 1 else 4) + t - 1
        return remote(block, block, q_send.at[h, n], q_recv.at[h, n], to_y[side])

    def z_copy(h):
        block = kvbuf.at[h, zh, x]
        return remote(block, block, z_send.at[h], z_recv.at[h], to_z)

    def x_copy(h, other, step):
        block = kvbuf.at[h, 1 - zh if other else zh, x]
        n = 3 * other + (1, -1, 2).index(step)
        return remote(block, block, x_send.at[h, n], x_recv.at[h, n], to_x[step])

    started = []

    def start(copy):
        copy.start()
        started.append(copy)

    def q_pass(h, side, t):
        q_copy(h, side, t).wait_recv()
        start(q_copy(h, side, t + 1))

    def z_pass(h):
        z_copy(h).wait_recv()
        for step in (2, 1, -1):
            start(x_copy(h, 1, step))

    for h in range(HPD):
        start(z_copy(h))
    for h in range(HPD):
        start(q_copy(h, 1, 1))
        start(q_copy(h, -1, 1))
    for h in range(HPD):
        for step in (2, 1, -1):
            start(x_copy(h, 0, step))

    for copy in loads[early:]:
        copy.wait()
    rels = (0, -1, 1, -2, 2, -3, 3, -4)
    slots = [mod(a + rel * way, NY) for rel in rels]
    lane = lax.broadcasted_iota(jnp.int32, (TOK, TOK), 1)
    row = lax.broadcasted_iota(jnp.int32, (TOK, TOK), 0)
    tile_lane, tile_row = lane[:NY], row[:NY]

    def by_row(scalars):
        tile = jnp.full((NY, TOK), scalars[0])
        for i in range(1, NY):
            tile = jnp.where(tile_row == i, scalars[i], tile)
        return tile

    query_spans = by_row([span_ref[slot_of(b, slot)] for slot in slots])
    for half in range(NZ):
        for j in range(NX):
            key_span = span_ref[slot_of(j * NZ + (zh if half == 0 else 1 - zh), a)]
            live = jnp.where(key_span <= query_spans, valid_ref[key_span], 0)
            bias[half, :, j * TOK : (j + 1) * TOK] = jnp.where(tile_lane < live, 0.0, EXCLUDED)

    for h in range(HPD):
        q_pass(h, 1, 1)
        q_pass(h, -1, 1)

    vwbuf[:, :, :, TOK:] = jnp.ones((HPD, NZ, HALF, TOK), jnp.bfloat16)
    my_spans = [span_ref[slot_of(b, i)] for i in range(NY)]
    live = by_row([valid_ref[span] for span in my_spans])
    step_rows = jnp.where(tile_lane < live, by_row([step_ref[span] for span in my_spans]), 0.0)
    order = jnp.broadcast_to(order_ref[...].astype(jnp.float32), (TOK, TOK))
    pick = (jnp.transpose(order) == lane.astype(jnp.float32)).astype(jnp.bfloat16)
    halves = (lane == 2 * lax.rem(row, PAIRS) + lax.div(row, PAIRS)).astype(jnp.bfloat16)
    pick = dot(halves, pick)
    lat = dot(pick.astype(jnp.bfloat16), lat_ref[...], ROWS_BY_KEYS)
    lat = jnp.where(g == 0, jnp.concatenate([lat[:PAIRS], lat[PAIRS:]], axis=1), 0.0)

    for h in range(HPD):
        q_pass(h, 1, 2)
        q_pass(h, -1, 2)

    def load_vw(h, half):
        for j in range(NX):
            packed = kvbuf[h, zh if half == 0 else 1 - zh, j, TOK:]
            for part in range(2):
                rows = slice(j * TOK + part * PAIRS, j * TOK + (part + 1) * PAIRS)
                vw = packed[:, part * LAT : (part + 1) * LAT]
                vwbuf[h, half, rows, :TOK] = jnp.concatenate([vw, vw], axis=1)

    def scores_of(h, half, places, queries):
        keys = kvbuf[h, zh if half == 0 else 1 - zh, :, :TOK].reshape(HALF, HD)
        scores = dot(queries, keys, ROWS_BY_KEYS)
        return jnp.concatenate(
            [scores[i * TOK : (i + 1) * TOK] + bias[half, n : n + 1] for i, n in enumerate(places)], axis=0
        )

    def weigh(h, half, scores, top):
        return dot(jnp.exp2((scores - top) * SCALE).astype(jnp.bfloat16), vwbuf[h, half])

    def stacked(ref, h, places):
        return jnp.concatenate([ref[h, slots[n]] for n in places], axis=0)

    def row_max(scores):
        return jnp.max(scores, axis=1, keepdims=True)

    def attend_own(h, places):
        scores = scores_of(h, 0, places, stacked(qbuf, h, places))
        top = row_max(scores)
        out = weigh(h, 0, scores, top)
        for i, n in enumerate(places):
            acc[h, slots[n]] = out[i * TOK : (i + 1) * TOK]
            tops[h, slots[n]] = top[i * TOK : (i + 1) * TOK]

    def finish(h, places, top, out):
        total = out[:, TOK:]
        lse = top * SCALE + jnp.log2(total)
        out = (out[:, :TOK] / total).astype(jnp.bfloat16)
        for i, n in enumerate(places):
            obuf[h, slots[n]] = out[i * TOK : (i + 1) * TOK]
        return [lse[i * TOK : (i + 1) * TOK] for i in range(len(places))]

    def attend_others(h, places):
        scores = scores_of(h, 1, places, stacked(qbuf, h, places))
        before = stacked(tops, h, places)
        top = jnp.maximum(row_max(scores), before)
        out = weigh(h, 1, scores, top) + jnp.exp2((before - top) * SCALE) * stacked(acc, h, places)
        return finish(h, places, top, out)

    def attend_all(h, places):
        queries = stacked(qbuf, h, places)
        scores = [scores_of(h, half, places, queries) for half in range(NZ)]
        top = jnp.maximum(row_max(scores[0]), row_max(scores[1]))
        return finish(h, places, top, sum(weigh(h, half, scores[half], top) for half in range(NZ)))

    def lse_copy(h, rel):
        block = lsebuf.at[h, a]
        return remote(block, block, s_send.at[h], s_recv.at[h], (slot_of(b, mod(a + rel, NY)), g))

    def lse_all(h):
        block = lsebuf.at[h, : NY - 1]
        return remote(block, block, s_send.at[h], s_recv.at[h], to_y[1])

    def lse_send(h, columns, lanes):
        stats = jnp.zeros((TOK, TOK), jnp.float32)
        for column, index in zip(columns, lanes):
            stats = jnp.where(lane == index, column, stats)
        lsebuf[h, a] = jnp.transpose(stats)[:NY]
        for rel in (4, 3, 5, 2, 6, 1, 7):
            lse_copy(h, rel).start()

    for h in range(HPD):
        for step in (1, -1, 2):
            x_copy(h, 0, step).wait_recv()
        load_vw(h, 0)
        attend_own(h, (0, 1, 2))
        if h == 0:
            z_pass(0)
    for h in range(HPD):
        attend_own(h, (3, 4))
        if h == 0:
            z_pass(1)
    z_pass(2)
    for h in range(HPD):
        q_pass(h, 1, 3)
        q_copy(h, -1, 3).wait_recv()
    for h in range(HPD):
        attend_own(h, (5, 6))
    for h in range(HPD):
        for step in (1, -1, 2):
            x_copy(h, 1, step).wait_recv()
        load_vw(h, 1)
        columns = attend_others(h, (0, 1, 2, 3)) + attend_others(h, (4, 5, 6))
        lse_send(h, columns, slots[: NY - 1])
    columns = []
    for h in range(HPD):
        q_copy(h, 1, 4).wait_recv()
        columns += attend_all(h, (NY - 1,))
    lse_send(HPD, columns, range(HPD))

    for device in head_peers:
        pl.semaphore_signal(ready, inc=1, device_id=device, device_id_type=MESH)

    for h in range(HPD + 1):
        lse_all(h).wait_recv()
    shares = []
    for h in range(HPD):
        parts = [
            jnp.where(tile_row == (i + NY // 2) % NY, lsebuf[HPD, i, h : h + 1], lsebuf[h, i]) for i in range(NY)
        ]
        own = jnp.where(tile_row == mod(a + NY // 2, NY), lsebuf[HPD, a, h : h + 1], lsebuf[h, a])
        top = parts[0]
        for part in parts[1:]:
            top = jnp.maximum(top, part)
        total = sum(jnp.exp2(part - top) for part in parts)
        shares.append(jnp.exp2(own - top) / total * step_rows)
    for i in range(NY):
        left = jnp.concatenate([(pick * share[i : i + 1]).astype(jnp.bfloat16) for share in shares], axis=1)
        term = dot(left, jnp.concatenate([obuf[h, i] for h in range(HPD)], axis=0))
        term = jnp.where(lane[:PAIRS] < LAT, term[:PAIRS], term[PAIRS:]) + jnp.where(a == i, lat, 0.0)
        for gg in range(NG):
            sendbuf[gg % 2, gg // 2, pl.ds(i, NY, stride=NY)] = term[gg * NY : (gg + 1) * NY]

    pl.semaphore_wait(ready, len(head_peers))
    pair_copy = remote(sendbuf.at[1 - core], pairbuf, p_send, p_recv, to_core)
    pair_copy.start()
    pair_copy.wait_recv()
    pairbuf[...] = pairbuf[...] + sendbuf[core]

    def owner(aa):
        return pl.ds(pl.multiple_of(aa * NY, NY), NY)

    def c_copy(rel):
        aa, gg = partner(rel)
        return remote(pairbuf.at[lax.div(gg, 2), owner(aa)], c1buf.at[rel - 1], c_send, c_recv, (slot_of(b, aa), gg))

    for rel in range(1, NY * NL):
        c_copy(rel).start()
    sums = remote(c1buf, c1buf, c_send, c_recv, to_core)
    sums.wait_recv()
    ubuf[...] = pairbuf[zl, owner(a)] + jnp.sum(c1buf[...], axis=0)

    def d_copy(gg):
        return remote(ubuf, dbuf.at[b], d_send.at[gg], d_recv.at[b], (slot_of(g, a), gg))

    def own_target(gg):
        return jnp.logical_and(self_last, gg == g)

    for gg in range(NG):
        @pl.when(jnp.logical_not(own_target(gg)))
        def _():
            d_copy(gg).start()

    @pl.when(self_last)
    def _():
        dbuf[b] = ubuf[...]

    zeros = jnp.zeros((LAT, LAT), jnp.bfloat16)
    taps = []
    for k in range(KT):
        tap = conv_ref[k]
        taps.append(jnp.concatenate([tap, zeros], axis=1))
        taps.append(jnp.concatenate([zeros, tap], axis=1))
    taps = jnp.concatenate(taps, axis=0)
    time = lax.broadcasted_iota(jnp.int32, (NSLOT, NSLOT), 0)
    spans = jnp.broadcast_to(span_row_ref[...], (NSLOT, NSLOT))
    orders = [(spans == time - k).astype(jnp.bfloat16) for k in range(KT)]

    for copy in started:
        copy.wait_send()
    for h in range(HPD + 1):
        lse_all(h).wait_send()
    pair_copy.wait_send()
    sums.wait_send()

    for bb in range(NB):
        @pl.when(jnp.logical_not(jnp.logical_and(self_last, bb == b)))
        def _():
            remote(ubuf, dbuf.at[bb], d_send.at[0], d_recv.at[bb], to_z).wait_recv()
    updated = dbuf[...].reshape(NSLOT, 2 * LAT).astype(jnp.bfloat16)
    shifted = [dot(order, updated).astype(jnp.bfloat16) for order in orders]
    features = dot(jnp.concatenate(shifted, axis=1), taps).astype(jnp.bfloat16)
    for p in range(2):
        denoised_ref[p] = shifted[0][:, p * LAT : (p + 1) * LAT]
        features_ref[p] = features[:, p * LAT : (p + 1) * LAT]

    for gg in range(NG):
        @pl.when(jnp.logical_not(own_target(gg)))
        def _():
            d_copy(gg).wait_send()


def local(
    queries, keys, values, latents, out_weight, step_size, conv_weight, span_of_slot, valid_count, decoder_order
):
    vmem, anywhere = pl.BlockSpec(memory_space=pltpu.VMEM), pl.BlockSpec(memory_space=pl.ANY)
    dma = pltpu.SemaphoreType.DMA
    bf16, f32, i32 = jnp.bfloat16, jnp.float32, jnp.int32
    out = jax.ShapeDtypeStruct((2, NSLOT, LAT), bf16)
    return pl.pallas_call(
        kernel,
        out_shape=(out, out),
        in_specs=[anywhere] * 11,
        out_specs=(vmem, vmem),
        scratch_shapes=[
            pltpu.VMEM((TOK, HPD * HD), bf16),
            pltpu.VMEM((LAT, TOK), bf16),
            pltpu.VMEM((LAT, HPD * HD), bf16),
            pltpu.VMEM((KT, LAT, LAT), bf16),
            pltpu.VMEM((1, NSLOT), i32),
            pltpu.VMEM((1, TOK), i32),
            pltpu.SMEM((NSLOT,), i32),
            pltpu.SMEM((NSLOT,), i32),
            pltpu.SMEM((NSLOT,), f32),
            pltpu.VMEM((HPD, NY, TOK, HD), bf16),
            pltpu.VMEM((HPD, NZ, NX, TOK + PAIRS, HD), bf16),
            pltpu.VMEM((HPD, NZ, HALF, 2 * TOK), bf16),
            pltpu.VMEM((HPD, NY, TOK, 2 * TOK), f32),
            pltpu.VMEM((HPD, NY, TOK, 1), f32),
            pltpu.VMEM((HPD, NY, TOK, TOK), bf16),
            pltpu.VMEM((NZ, NY, HALF), f32),
            pltpu.VMEM((HPD + 1, NY, NY, TOK), f32),
            pltpu.VMEM((2, NL, NY * NY, TOK), f32),
            pltpu.VMEM((NL, NY * NY, TOK), f32),
            pltpu.VMEM((NY * NL - 1, NY, TOK), f32),
            pltpu.VMEM((NY, TOK), f32),
            pltpu.VMEM((NB, NY, TOK), f32),
            pltpu.SemaphoreType.REGULAR,
            dma((15,)),
            dma((HPD, 7)), dma((HPD, 7)),
            dma((HPD,)), dma((HPD,)),
            dma((HPD, 6)), dma((HPD, 6)),
            dma((HPD + 1,)), dma((HPD + 1,)),
            dma, dma,
            dma, dma,
            dma((NG,)), dma((NB,)),
        ],
        compiler_params=pltpu.CompilerParams(
            collective_id=0, has_side_effects=True, vmem_limit_bytes=54 * 2**20
        ),
        name="span_attention",
    )(
        queries, keys, values, latents.T, out_weight.T, conv_weight,
        span_of_slot.reshape(1, NSLOT), decoder_order.reshape(1, TOK),
        span_of_slot, valid_count, step_size,
    )


def solution(mesh):
    return jax.shard_map(
        local,
        mesh=mesh,
        in_specs=(
            P("tm", "head"),
            P("tm", "head"),
            P("tm", "head"),
            P("tm", None),
            P("head", None),
            P(),
            P(None, None, "head"),
            P(),
            P(),
            P(),
        ),
        out_specs=(P("tm", None, None), P("tm", None, "head")),
        check_vma=False,
    )
```

time: 63.4 us -> 57.2 us (0.902)
  Pallas kernels: 57.7 us -> 54.3 us
  local copies, waits for them, and re-layouts: 4.74 us -> 2 us
    pallas_call x1, Pallas kernels: 57.7 us -> 54.3 us  [local(): pl.pallas_call(kernel, out_shape=(out, out), in_specs=[anywhere] * 11, ou...]
    unnamed x20 -> x4, local copies, waits for them, and re-layouts: 4.74 us -> 2 us
where the time goes in v2:
time: 57.2 us; the launch traced here: 56.9 us
  Pallas kernels  54.3 us (95%)
  local copies, waits for them, and re-layouts  2 us (3%)
  between operations  0.65 us (1%)
    pallas_call x1, Pallas kernels, local(): pl.pallas_call(kernel, out_shape=(out, out), in_specs=[anywhere] * 11, ou...  54.3 us
    unnamed x4, local copies, waits for them, and re-layouts  2 us

profile of v2, /device:TPU:1, one launch (start us, length us, event | category | flops | bytes accessed | tf_op | source)
XLA Modules:
  0.0 56.9 jit_solution(12130542023622001709)
XLA Ops:
  0.6 54.3 %span_attention.1 = (bf16[2,64,64]{2,1,0:T(8,128)(2,1)}, bf16[2,64,64]{2,1,0:T(8,128)(2,1)}) custom-call(bf16[128,384]{1,0:T(8,128)(2,1)} %q_hbm.1, bf16[128,384]{1,0:T(8,128)(2,1)} %k_hbm.1, bf16[128,384]{1,0:T(8,128)(2,1)} %v_hbm.1, bf16[64,128]{1,0:T(8,128)(2,1)} %bitcast.5, bf16[64,384]{1,0:T(8,128)(2,1)} %bitcast.4, bf16[3,64,64]{2,1,0:T(8,128)(2,1)} %conv_hbm.1, ...), custom_call_target="tpu_custom_call" | custom-call | tf_op jit(solution)/shard_map/span_attention/pallas_call | solution.py:380
  54.9 0.0 copy-start
  55.0 1.4 %copy.14 = bf16[2,64,64]{2,1,0:T(8,128)(2,1)} copy(bf16[2,64,64]{2,1,0:T(8,128)(2,1)} %get-tuple-element.4) | data formatting | bytes 32768
  56.3 0.0 copy-done
  56.3 0.6 %copy.15 = bf16[2,64,64]{2,1,0:T(8,128)(2,1)} copy(bf16[2,64,64]{2,1,0:T(8,128)(2,1)S(1)} %copy-done) | data formatting | bytes 32768
Async XLA Ops:
  54.9 1.4 %copy-start = (bf16[2,64,64]{2,1,0:T(8,128)(2,1)S(1)}, bf16[2,64,64]{2,1,0:T(8,128)(2,1)}, u32[]{:S(2)}) copy-start(bf16[2,64,64]{2,1,0:T(8,128)(2,1)} %get-tuple-element.5) | copy-start | bytes 49156

commit v3 on v2

--- a/solution.py
+++ b/solution.py
@@ -39,9 +39,9 @@
 
 def kernel(
     q_hbm, k_hbm, v_hbm, lat_hbm, wout_hbm, conv_hbm, span_row_hbm, order_hbm, span_hbm, valid_hbm, step_hbm,
-    denoised_ref, features_ref,
+    out_ref,
     v_ref, lat_ref, wout_ref, conv_ref, span_row_ref, order_ref, span_ref, valid_ref, step_ref,
-    qbuf, kvbuf, vwbuf, acc, tops, obuf, bias, lsebuf, sendbuf, pairbuf, c1buf, ubuf, dbuf,
+    qbuf, kvbuf, vwbuf, acc, tops, obuf, bias, lsebuf, stage, sendbuf, c1buf, sumbuf, pairbuf, ubuf, dbuf,
     ready, load, q_send, q_recv, z_send, z_recv, x_send, x_recv, s_send, s_recv,
     p_send, p_recv, c_send, c_recv, d_send, d_recv,
 ):
@@ -55,7 +55,7 @@
     def slot_of(bb, aa):
         return bb * NY + aa
 
-    to_y = {s: (slot_of(b, mod(a + s * way, NY)), g) for s in (1, -1)}
+    to_y = {s: (slot_of(b, mod(a + s * way, NY)), g) for s in (1, -1, 2, -2)}
     to_x = {s: (slot_of(mod(x + s, NX) * NZ + zh, a), g) for s in (1, -1, 2)}
     to_z = (slot_of(x * NZ + 1 - zh, a), g)
     to_core = (tm, g + way)
@@ -63,7 +63,7 @@
 
     barrier = pltpu.get_barrier_semaphore()
     head_peers = [(tm, mod(g + rel, NG)) for rel in range(1, NG)]
-    greeted = [to_z, to_x[1], to_x[-1], to_x[2], to_y[1], to_y[-1], *head_peers]
+    greeted = [to_z, to_x[1], to_x[-1], to_x[2], *to_y.values(), *head_peers]
     for device in greeted:
         pl.semaphore_signal(barrier, inc=1, device_id=device, device_id_type=MESH)
 
@@ -102,17 +102,20 @@
 
     pl.semaphore_wait(barrier, len(greeted))
 
-    def q_copy(h, side, t):
-        block = qbuf.at[h, mod(a - side * way * (t - 1), NY)]
-        n = (0 if side == 1 else 4) + t - 1
-        return remote(block, block, q_send.at[h, n], q_recv.at[h, n], to_y[side])
+    def q_copy(h, side, distance, hop):
+        block = qbuf.at[h, mod(a - side * way * (distance - hop), NY)]
+        n = (0 if side == 1 else 4) + distance - 1
+        return remote(block, block, q_send.at[h, n], q_recv.at[h, n], to_y[side * hop])
+
+    def q_wait(h, side, distance):
+        q_copy(h, side, distance, min(distance, 2)).wait_recv()
 
     def z_copy(h):
         block = kvbuf.at[h, zh, x]
         return remote(block, block, z_send.at[h], z_recv.at[h], to_z)
 
     def x_copy(h, other, step):
-        block = kvbuf.at[h, 1 - zh if other else zh, x]
+        block = kvbuf.at[h, 1 - zh, x] if other else kvbuf.at[:, zh, x]
         n = 3 * other + (1, -1, 2).index(step)
         return remote(block, block, x_send.at[h, n], x_recv.at[h, n], to_x[step])
 
@@ -122,9 +125,12 @@
         copy.start()
         started.append(copy)
 
-    def q_pass(h, side, t):
-        q_copy(h, side, t).wait_recv()
-        start(q_copy(h, side, t + 1))
+    def q_pass(h):
+        q_wait(h, 1, 2)
+        start(q_copy(h, 1, 4, 2))
+        start(q_copy(h, 1, 3, 1))
+        q_wait(h, -1, 2)
+        start(q_copy(h, -1, 3, 1))
 
     def z_pass(h):
         z_copy(h).wait_recv()
@@ -134,11 +140,13 @@
     for h in range(HPD):
         start(z_copy(h))
     for h in range(HPD):
-        start(q_copy(h, 1, 1))
-        start(q_copy(h, -1, 1))
-    for h in range(HPD):
-        for step in (2, 1, -1):
-            start(x_copy(h, 0, step))
+        for side in (1, -1):
+            start(q_copy(h, side, 2, 2))
+    for step in (2, 1, -1):
+        start(x_copy(0, 0, step))
+    for h in range(HPD):
+        for side in (1, -1):
+            start(q_copy(h, side, 1, 1))
 
     for copy in loads[early:]:
         copy.wait()
@@ -160,10 +168,6 @@
             key_span = span_ref[slot_of(j * NZ + (zh if half == 0 else 1 - zh), a)]
             live = jnp.where(key_span <= query_spans, valid_ref[key_span], 0)
             bias[half, :, j * TOK : (j + 1) * TOK] = jnp.where(tile_lane < live, 0.0, EXCLUDED)
-
-    for h in range(HPD):
-        q_pass(h, 1, 1)
-        q_pass(h, -1, 1)
 
     vwbuf[:, :, :, TOK:] = jnp.ones((HPD, NZ, HALF, TOK), jnp.bfloat16)
     my_spans = [span_ref[slot_of(b, i)] for i in range(NY)]
@@ -177,8 +181,9 @@
     lat = jnp.where(g == 0, jnp.concatenate([lat[:PAIRS], lat[PAIRS:]], axis=1), 0.0)
 
     for h in range(HPD):
-        q_pass(h, 1, 2)
-        q_pass(h, -1, 2)
+        q_pass(h)
+    for h in range(HPD):
+        z_pass(h)
 
     def load_vw(h, half):
         for j in range(NX):
@@ -241,84 +246,76 @@
         block = lsebuf.at[h, : NY - 1]
         return remote(block, block, s_send.at[h], s_recv.at[h], to_y[1])
 
-    def lse_send(h, columns, lanes):
+    def lse_send(h, columns, places):
         stats = jnp.zeros((TOK, TOK), jnp.float32)
-        for column, index in zip(columns, lanes):
+        for column, index in zip(columns, [slots[n] for n in places]):
             stats = jnp.where(lane == index, column, stats)
         lsebuf[h, a] = jnp.transpose(stats)[:NY]
         for rel in (4, 3, 5, 2, 6, 1, 7):
             lse_copy(h, rel).start()
 
-    for h in range(HPD):
-        for step in (1, -1, 2):
-            x_copy(h, 0, step).wait_recv()
+    for step in (1, -1, 2):
+        x_copy(0, 0, step).wait_recv()
+    for h in range(HPD):
         load_vw(h, 0)
+        q_wait(h, 1, 1)
+        q_wait(h, -1, 1)
         attend_own(h, (0, 1, 2))
-        if h == 0:
-            z_pass(0)
-    for h in range(HPD):
         attend_own(h, (3, 4))
-        if h == 0:
-            z_pass(1)
-    z_pass(2)
-    for h in range(HPD):
-        q_pass(h, 1, 3)
-        q_copy(h, -1, 3).wait_recv()
-    for h in range(HPD):
-        attend_own(h, (5, 6))
+    for h in range(HPD):
+        q_wait(h, 1, 3)
+        q_wait(h, -1, 3)
+        q_wait(h, 1, 4)
+    for h in range(HPD):
+        attend_own(h, (5, 6, 7))
     for h in range(HPD):
         for step in (1, -1, 2):
             x_copy(h, 1, step).wait_recv()
         load_vw(h, 1)
-        columns = attend_others(h, (0, 1, 2, 3)) + attend_others(h, (4, 5, 6))
-        lse_send(h, columns, slots[: NY - 1])
-    columns = []
-    for h in range(HPD):
-        q_copy(h, 1, 4).wait_recv()
-        columns += attend_all(h, (NY - 1,))
-    lse_send(HPD, columns, range(HPD))
+        columns = attend_others(h, (0, 1, 2, 3)) + attend_others(h, (4, 5, 6, 7))
+        lse_send(h, columns, range(NY))
 
     for device in head_peers:
         pl.semaphore_signal(ready, inc=1, device_id=device, device_id_type=MESH)
 
-    for h in range(HPD + 1):
+    for h in range(HPD):
         lse_all(h).wait_recv()
     shares = []
     for h in range(HPD):
-        parts = [
-            jnp.where(tile_row == (i + NY // 2) % NY, lsebuf[HPD, i, h : h + 1], lsebuf[h, i]) for i in range(NY)
-        ]
-        own = jnp.where(tile_row == mod(a + NY // 2, NY), lsebuf[HPD, a, h : h + 1], lsebuf[h, a])
-        top = parts[0]
-        for part in parts[1:]:
-            top = jnp.maximum(top, part)
-        total = sum(jnp.exp2(part - top) for part in parts)
-        shares.append(jnp.exp2(own - top) / total * step_rows)
+        parts = lsebuf[h]
+        top = jnp.max(parts, axis=0)
+        total = jnp.sum(jnp.exp2(parts - top[None]), axis=0)
+        shares.append(jnp.exp2(lsebuf[h, a] - top) / total * step_rows)
     for i in range(NY):
         left = jnp.concatenate([(pick * share[i : i + 1]).astype(jnp.bfloat16) for share in shares], axis=1)
         term = dot(left, jnp.concatenate([obuf[h, i] for h in range(HPD)], axis=0))
         term = jnp.where(lane[:PAIRS] < LAT, term[:PAIRS], term[PAIRS:]) + jnp.where(a == i, lat, 0.0)
         for gg in range(NG):
-            sendbuf[gg % 2, gg // 2, pl.ds(i, NY, stride=NY)] = term[gg * NY : (gg + 1) * NY]
+            stage[gg // 2, pl.ds(gg % 2 * NY + i, NY, stride=2 * NY)] = term[gg * NY : (gg + 1) * NY]
+    sendbuf[...] = stage[...].astype(jnp.bfloat16)
 
     pl.semaphore_wait(ready, len(head_peers))
-    pair_copy = remote(sendbuf.at[1 - core], pairbuf, p_send, p_recv, to_core)
-    pair_copy.start()
-    pair_copy.wait_recv()
-    pairbuf[...] = pairbuf[...] + sendbuf[core]
 
     def owner(aa):
-        return pl.ds(pl.multiple_of(aa * NY, NY), NY)
+        return pl.ds(pl.multiple_of(aa * 2 * NY, 2 * NY), 2 * NY)
 
     def c_copy(rel):
         aa, gg = partner(rel)
-        return remote(pairbuf.at[lax.div(gg, 2), owner(aa)], c1buf.at[rel - 1], c_send, c_recv, (slot_of(b, aa), gg))
-
-    for rel in range(1, NY * NL):
+        return remote(sendbuf.at[lax.div(gg, 2), owner(aa)], c1buf.at[rel - 1], c_send, c_recv, (slot_of(b, aa), gg))
+
+    def hops(rel):
+        return min(rel // NL, NY - rel // NL) + min(rel % NL, NL - rel % NL)
+
+    for rel in sorted(range(1, NY * NL), key=hops, reverse=True):
         c_copy(rel).start()
     sums = remote(c1buf, c1buf, c_send, c_recv, to_core)
     sums.wait_recv()
-    ubuf[...] = pairbuf[zl, owner(a)] + jnp.sum(c1buf[...], axis=0)
+    total = stage[zl, owner(a)] + jnp.sum(c1buf[...].astype(jnp.float32), axis=0)
+    sumbuf[...] = total.reshape(2, NY, TOK)
+    pair_copy = remote(sumbuf.at[1 - core], pairbuf, p_send, p_recv, to_core)
+    pair_copy.start()
+    pair_copy.wait_recv()
+    ubuf[...] = sumbuf[core] + pairbuf[...]
 
     def d_copy(gg):
         return remote(ubuf, dbuf.at[b], d_send.at[gg], d_recv.at[b], (slot_of(g, a), gg))
@@ -348,7 +345,7 @@
 
     for copy in started:
         copy.wait_send()
-    for h in range(HPD + 1):
+    for h in range(HPD):
         lse_all(h).wait_send()
     pair_copy.wait_send()
     sums.wait_send()
@@ -360,9 +357,10 @@
     updated = dbuf[...].reshape(NSLOT, 2 * LAT).astype(jnp.bfloat16)
     shifted = [dot(order, updated).astype(jnp.bfloat16) for order in orders]
     features = dot(jnp.concatenate(shifted, axis=1), taps).astype(jnp.bfloat16)
+    denoised = shifted[0]
     for p in range(2):
-        denoised_ref[p] = shifted[0][:, p * LAT : (p + 1) * LAT]
-        features_ref[p] = features[:, p * LAT : (p + 1) * LAT]
+        part = slice(p * LAT, (p + 1) * LAT)
+        out_ref[p] = jnp.concatenate([denoised[:, part], features[:, part]], axis=1)
 
     for gg in range(NG):
         @pl.when(jnp.logical_not(own_target(gg)))
@@ -376,12 +374,11 @@
     vmem, anywhere = pl.BlockSpec(memory_space=pltpu.VMEM), pl.BlockSpec(memory_space=pl.ANY)
     dma = pltpu.SemaphoreType.DMA
     bf16, f32, i32 = jnp.bfloat16, jnp.float32, jnp.int32
-    out = jax.ShapeDtypeStruct((2, NSLOT, LAT), bf16)
-    return pl.pallas_call(
+    both = pl.pallas_call(
         kernel,
-        out_shape=(out, out),
+        out_shape=jax.ShapeDtypeStruct((2, NSLOT, 2 * LAT), bf16),
         in_specs=[anywhere] * 11,
-        out_specs=(vmem, vmem),
+        out_specs=vmem,
         scratch_shapes=[
             pltpu.VMEM((TOK, HPD * HD), bf16),
             pltpu.VMEM((LAT, TOK), bf16),
@@ -399,10 +396,12 @@
             pltpu.VMEM((HPD, NY, TOK, 1), f32),
             pltpu.VMEM((HPD, NY, TOK, TOK), bf16),
             pltpu.VMEM((NZ, NY, HALF), f32),
-            pltpu.VMEM((HPD + 1, NY, NY, TOK), f32),
-            pltpu.VMEM((2, NL, NY * NY, TOK), f32),
-            pltpu.VMEM((NL, NY * NY, TOK), f32),
-            pltpu.VMEM((NY * NL - 1, NY, TOK), f32),
+            pltpu.VMEM((HPD, NY, NY, TOK), f32),
+            pltpu.VMEM((NL, 2 * NY * NY, TOK), f32),
+            pltpu.VMEM((NL, 2 * NY * NY, TOK), bf16),
+            pltpu.VMEM((NY * NL - 1, 2 * NY, TOK), bf16),
+            pltpu.VMEM((2, NY, TOK), f32),
+            pltpu.VMEM((NY, TOK), f32),
             pltpu.VMEM((NY, TOK), f32),
             pltpu.VMEM((NB, NY, TOK), f32),
             pltpu.SemaphoreType.REGULAR,
@@ -410,7 +409,7 @@
             dma((HPD, 7)), dma((HPD, 7)),
             dma((HPD,)), dma((HPD,)),
             dma((HPD, 6)), dma((HPD, 6)),
-            dma((HPD + 1,)), dma((HPD + 1,)),
+            dma((HPD,)), dma((HPD,)),
             dma, dma,
             dma, dma,
             dma((NG,)), dma((NB,)),
@@ -424,6 +423,7 @@
         span_of_slot.reshape(1, NSLOT), decoder_order.reshape(1, TOK),
         span_of_slot, valid_count, step_size,
     )
+    return both[:, :, :LAT], both[:, :, LAT:]
 
 
 def solution(mesh):

time: 57.2 us -> 55.3 us (0.967)
  Pallas kernels: 54.3 us -> 52.9 us
    unnamed x4 -> x0, local copies, waits for them, and re-layouts: 2 us -> none
    slice x0 -> x1, local copies, waits for them, and re-layouts: none -> 1.53 us  [local(): return (both[:, :, :LAT], both[:, :, LAT:])]
    pallas_call x1, Pallas kernels: 54.3 us -> 52.9 us  [local(): pl.pallas_call(kernel, out_shape=jax.ShapeDtypeStruct((2, NSLOT, 2 * LAT)...]
where the time goes in v3:
time: 55.3 us; the launch traced here: 55 us
  Pallas kernels  52.9 us (96%)
  local copies, waits for them, and re-layouts  1.53 us (3%)
  between operations  0.64 us (1%)
    pallas_call x1, Pallas kernels, local(): pl.pallas_call(kernel, out_shape=jax.ShapeDtypeStruct((2, NSLOT, 2 * LAT)...  52.9 us
    slice x1, local copies, waits for them, and re-layouts, local(): return (both[:, :, :LAT], both[:, :, LAT:])  1.53 us

profile of v3, /device:TPU:1, one launch (start us, length us, event | category | flops | bytes accessed | tf_op | source)
XLA Modules:
  0.0 55.0 jit_solution(17868223518059185094)
XLA Ops:
  0.6 52.9 %span_attention.1 = bf16[2,64,128]{2,1,0:T(8,128)(2,1)} custom-call(bf16[128,384]{1,0:T(8,128)(2,1)} %q_hbm.1, bf16[128,384]{1,0:T(8,128)(2,1)} %k_hbm.1, bf16[128,384]{1,0:T(8,128)(2,1)} %v_hbm.1, bf16[64,128]{1,0:T(8,128)(2,1)} %bitcast.5, bf16[64,384]{1,0:T(8,128)(2,1)} %bitcast.4, bf16[3,64,64]{2,1,0:T(8,128)(2,1)} %conv_hbm.1, s32[1,64]{1,0:T(1,128)} %bitcast.6, ...), custom_call_target="tpu_custom_call" | custom-call | tf_op jit(solution)/shard_map/span_attention/pallas_call | solution.py:377
  53.5 1.5 %fusion = (bf16[2,64,64]{2,1,0:T(8,128)(2,1)}, bf16[2,64,64]{2,1,0:T(8,128)(2,1)}) fusion(bf16[2,64,128]{2,1,0:T(8,128)(2,1)} %span_attention.1), kind=kLoop, calls=%fused_computation | loop fusion | bytes 65536 | tf_op jit(solution)/shard_map/slice | solution.py:426

commit v4 on v3

--- a/solution.py
+++ b/solution.py
@@ -80,24 +80,19 @@
     def cols(h):
         return slice(h * HD, (h + 1) * HD)
 
+    for h in range(HPD):
+        fetch(q_hbm.at[:, cols(h)], qbuf.at[h, a])
     fetch(v_hbm, v_ref)
     fetch(wout_hbm, wout_ref)
     for h in range(HPD):
         fetch(k_hbm.at[:, cols(h)], kvbuf.at[h, zh, x, :TOK])
-    for h in range(HPD):
-        fetch(q_hbm.at[:, cols(h)], qbuf.at[h, a])
     early = len(loads)
     for src, dst in (
         (span_hbm, span_ref), (valid_hbm, valid_ref), (step_hbm, step_ref), (span_row_hbm, span_row_ref),
         (order_hbm, order_ref), (lat_hbm, lat_ref), (conv_hbm, conv_ref),
     ):
         fetch(src, dst)
-    for copy in loads[:2]:
-        copy.wait()
-    for h in range(HPD):
-        vw = dot(v_ref[:, cols(h)], wout_ref[:, cols(h)], ROWS_BY_KEYS)
-        kvbuf[h, zh, x, TOK:] = jnp.concatenate([vw[:PAIRS], vw[PAIRS:]], axis=1).astype(jnp.bfloat16)
-    for copy in loads[2:early]:
+    for copy in loads[:HPD]:
         copy.wait()
 
     pl.semaphore_wait(barrier, len(greeted))
@@ -138,10 +133,17 @@
             start(x_copy(h, 1, step))
 
     for h in range(HPD):
-        start(z_copy(h))
-    for h in range(HPD):
         for side in (1, -1):
             start(q_copy(h, side, 2, 2))
+    for copy in loads[HPD : HPD + 2]:
+        copy.wait()
+    for h in range(HPD):
+        vw = dot(v_ref[:, cols(h)], wout_ref[:, cols(h)], ROWS_BY_KEYS)
+        kvbuf[h, zh, x, TOK:] = jnp.concatenate([vw[:PAIRS], vw[PAIRS:]], axis=1).astype(jnp.bfloat16)
+    for copy in loads[HPD + 2 : early]:
+        copy.wait()
+    for h in range(HPD):
+        start(z_copy(h))
     for step in (2, 1, -1):
         start(x_copy(0, 0, step))
     for h in range(HPD):
@@ -260,8 +262,8 @@
         load_vw(h, 0)
         q_wait(h, 1, 1)
         q_wait(h, -1, 1)
-        attend_own(h, (0, 1, 2))
-        attend_own(h, (3, 4))
+        attend_own(h, (0, 1))
+        attend_own(h, (2, 3, 4))
     for h in range(HPD):
         q_wait(h, 1, 3)
         q_wait(h, -1, 3)
@@ -272,7 +274,7 @@
         for step in (1, -1, 2):
             x_copy(h, 1, step).wait_recv()
         load_vw(h, 1)
-        columns = attend_others(h, (0, 1, 2, 3)) + attend_others(h, (4, 5, 6, 7))
+        columns = sum((attend_others(h, (2 * n, 2 * n + 1)) for n in range(NY // 2)), [])
         lse_send(h, columns, range(NY))
 
     for device in head_peers:

time: 55.3 us -> 54.9 us (level)
  no operation moved by 1% of the time
where the time goes in v4:
time: 54.9 us; the launch traced here: 54.7 us
  Pallas kernels  52.5 us (96%)
  local copies, waits for them, and re-layouts  1.53 us (3%)
  between operations  0.64 us (1%)
    pallas_call x1, Pallas kernels, local(): pl.pallas_call(kernel, out_shape=jax.ShapeDtypeStruct((2, NSLOT, 2 * LAT)...  52.5 us
    slice x1, local copies, waits for them, and re-layouts, local(): return (both[:, :, :LAT], both[:, :, LAT:])  1.53 us

profile of v4, /device:TPU:1, one launch (start us, length us, event | category | flops | bytes accessed | tf_op | source)
XLA Modules:
  0.0 54.7 jit_solution(10771675155673716300)
XLA Ops:
  0.6 52.5 %span_attention.1 = bf16[2,64,128]{2,1,0:T(8,128)(2,1)} custom-call(bf16[128,384]{1,0:T(8,128)(2,1)} %q_hbm.1, bf16[128,384]{1,0:T(8,128)(2,1)} %k_hbm.1, bf16[128,384]{1,0:T(8,128)(2,1)} %v_hbm.1, bf16[64,128]{1,0:T(8,128)(2,1)} %bitcast.5, bf16[64,384]{1,0:T(8,128)(2,1)} %bitcast.4, bf16[3,64,64]{2,1,0:T(8,128)(2,1)} %conv_hbm.1, s32[1,64]{1,0:T(1,128)} %bitcast.6, ...), custom_call_target="tpu_custom_call" | custom-call | tf_op jit(solution)/shard_map/span_attention/pallas_call | solution.py:379
  53.2 1.5 %fusion = (bf16[2,64,64]{2,1,0:T(8,128)(2,1)}, bf16[2,64,64]{2,1,0:T(8,128)(2,1)}) fusion(bf16[2,64,128]{2,1,0:T(8,128)(2,1)} %span_attention.1), kind=kLoop, calls=%fused_computation | loop fusion | bytes 65536 | tf_op jit(solution)/shard_map/slice | solution.py:428

commit v5 on v4

--- a/solution.py
+++ b/solution.py
@@ -178,8 +178,8 @@
     order = jnp.broadcast_to(order_ref[...].astype(jnp.float32), (TOK, TOK))
     pick = (jnp.transpose(order) == lane.astype(jnp.float32)).astype(jnp.bfloat16)
     halves = (lane == 2 * lax.rem(row, PAIRS) + lax.div(row, PAIRS)).astype(jnp.bfloat16)
-    pick = dot(halves, pick)
-    lat = dot(pick.astype(jnp.bfloat16), lat_ref[...], ROWS_BY_KEYS)
+    pick = dot(halves, pick).astype(jnp.bfloat16)
+    lat = dot(pick, lat_ref[...], ROWS_BY_KEYS)
     lat = jnp.where(g == 0, jnp.concatenate([lat[:PAIRS], lat[PAIRS:]], axis=1), 0.0)
 
     for h in range(HPD):
@@ -289,7 +289,7 @@
         total = jnp.sum(jnp.exp2(parts - top[None]), axis=0)
         shares.append(jnp.exp2(lsebuf[h, a] - top) / total * step_rows)
     for i in range(NY):
-        left = jnp.concatenate([(pick * share[i : i + 1]).astype(jnp.bfloat16) for share in shares], axis=1)
+        left = jnp.concatenate([pick * share[i : i + 1].astype(jnp.bfloat16) for share in shares], axis=1)
         term = dot(left, jnp.concatenate([obuf[h, i] for h in range(HPD)], axis=0))
         term = jnp.where(lane[:PAIRS] < LAT, term[:PAIRS], term[PAIRS:]) + jnp.where(a == i, lat, 0.0)
         for gg in range(NG):

time: 54.9 us -> 54.9 us (level)
  no operation moved by 1% of the time
where the time goes in v5:
time: 54.9 us; the launch traced here: 54.7 us
  Pallas kernels  52.5 us (96%)
  local copies, waits for them, and re-layouts  1.53 us (3%)
  between operations  0.64 us (1%)
    pallas_call x1, Pallas kernels, local(): pl.pallas_call(kernel, out_shape=jax.ShapeDtypeStruct((2, NSLOT, 2 * LAT)...  52.5 us
    slice x1, local copies, waits for them, and re-layouts, local(): return (both[:, :, :LAT], both[:, :, LAT:])  1.53 us

profile of v5, /device:TPU:1, one launch (start us, length us, event | category | flops | bytes accessed | tf_op | source)
XLA Modules:
  0.0 54.7 jit_solution(15707761251940392917)
XLA Ops:
  0.6 52.5 %span_attention.1 = bf16[2,64,128]{2,1,0:T(8,128)(2,1)} custom-call(bf16[128,384]{1,0:T(8,128)(2,1)} %q_hbm.1, bf16[128,384]{1,0:T(8,128)(2,1)} %k_hbm.1, bf16[128,384]{1,0:T(8,128)(2,1)} %v_hbm.1, bf16[64,128]{1,0:T(8,128)(2,1)} %bitcast.5, bf16[64,384]{1,0:T(8,128)(2,1)} %bitcast.4, bf16[3,64,64]{2,1,0:T(8,128)(2,1)} %conv_hbm.1, s32[1,64]{1,0:T(1,128)} %bitcast.6, ...), custom_call_target="tpu_custom_call" | custom-call | tf_op jit(solution)/shard_map/span_attention/pallas_call | solution.py:379
  53.2 1.5 %fusion = (bf16[2,64,64]{2,1,0:T(8,128)(2,1)}, bf16[2,64,64]{2,1,0:T(8,128)(2,1)}) fusion(bf16[2,64,128]{2,1,0:T(8,128)(2,1)} %span_attention.1), kind=kLoop, calls=%fused_computation | loop fusion | bytes 65536 | tf_op jit(solution)/shard_map/slice | solution.py:428
